TPU v7x, 32 devices: a whole 2x2x4 slice. The times are simulated.
32 devices in a mesh: dp: 2 (over x), tp: 16 (over z, y, core).
Axes of the slice: x: 2, y: 2, z: 4, core: 2. Of those that a mesh axis runs over, the one named last changes fastest.
Arguments:
- hidden: bfloat16 [512, 26624], P('dp', 'tp'), may hold values from -0.25 to 0.25
- out_grad: bfloat16 [512, 8192], P(('dp', 'tp')), may hold values from -6 to 6
- down_weight: bfloat16 [26624, 8192], P('tp', 'dp'), may hold values from -0.0625 to 0.0625
Outputs:
- input_grad: bfloat16 [512, 26624], P('dp', 'tp')
- weight_grad: bfloat16 [26624, 8192], P('tp', 'dp')
All inputs are finite; a program needn't handle non-finite values.
Results may differ from a plain program's by a relative error of at most 0.009.
Values may be sent and summed in bfloat16 or wider, within the bound.
A program may use at most 128 MiB of HBM per device.

v0:
```python
import jax
import jax.numpy as jnp
from jax import lax
from jax.sharding import PartitionSpec as P


def shards(hidden, out_grad, down_weight):
    whole_weight = lax.all_gather(down_weight, "dp", axis=1, tiled=True)
    row_count = hidden.shape[0]
    unit_count = hidden.shape[1]
    received = lax.all_gather(out_grad, "tp", axis=0, tiled=True)
    block = lax.dot_general(
        received, whole_weight, (((1,), (1,)), ((), ())), preferred_element_type=jnp.float32
    )
    token_blocks = lax.all_to_all(received, "dp", split_axis=1, concat_axis=0, tiled=True)
    hidden_all = lax.all_gather(hidden, "dp", axis=0, tiled=True)
    group_count = lax.axis_size("dp")
    hidden_groups = hidden_all.reshape(group_count, row_count, unit_count)
    grad_groups = token_blocks.reshape(group_count, row_count, token_blocks.shape[1])
    partials = jnp.einsum(
        "gtf,gtd->gfd", hidden_groups, grad_groups, preferred_element_type=jnp.float32
    ).astype(jnp.bfloat16)
    weight_grad = jnp.sum(partials.astype(jnp.float32), axis=0).astype(jnp.bfloat16)
    return (block.astype(jnp.bfloat16), weight_grad)


def solution(mesh):
    placed = (P("dp", "tp"), P(("dp", "tp"), None), P("tp", "dp"))
    return jax.shard_map(
        shards,
        mesh=mesh,
        in_specs=placed,
        out_specs=(P("dp", "tp"), P("tp", "dp")),
        check_vma=False,
    )
```

profile of v0, /device:TPU:0, one launch (start us, length us, event | category | flops | bytes accessed | tf_op | source)
XLA Modules:
  0.0 450.7 jit_solution(11598344002066745449)
XLA Ops:
  7.2 0.0 all-gather.4.cloned.1.call-start
  7.2 0.7 all-gather.4.cloned.1.call-update
  7.9 0.0 all-gather.8.cloned.1.call-start
  7.9 0.7 all-gather.8.cloned.1.call-update
  8.6 0.0 all-gather.6.cloned.1.call-start
  8.7 0.7 all-gather.6.cloned.1.call-update
  9.4 54.1 %all-gather.4.cloned.1.call-done = bf16[256,8192]{1,0:T(8,128)(2,1)} async-done(((bf16[16,8192]{1,0:T(8,128)(2,1)}), bf16[256,8192]{1,0:T(8,128)(2,1)}) %all-gather.4.cloned.1.call-update) | async-done | bytes 4194320 | tf_op jit(solution)/shard_map/all_gather | solution.py:11
  63.5 6.4 %copy.8 = bf16[256,8192]{0,1:T(8,128)(2,1)} copy(bf16[256,8192]{1,0:T(8,128)(2,1)} %all-gather.4.cloned.1.call-done) | data formatting | bytes 8388608 | tf_op jit(solution)/shard_map/all_gather | solution.py:11
  69.8 6.5 %copy.9 = bf16[256,2,4096]{2,0,1:T(8,128)(2,1)} copy(bf16[256,2,4096]{0,2,1:T(8,128)(2,1)} %bitcast.8) | data formatting | bytes 8388608 | tf_op jit(solution)/shard_map/all_to_all | solution.py:15
  76.3 5.6 %all-to-all-start = ((bf16[256,2,4096]{2,0,1:T(8,128)(2,1)}), bf16[256,2,4096]{2,0,1:T(8,128)(2,1)}, u32[]{:S(2)}, u32[]{:S(2)}) async-start(bf16[256,2,4096]{2,0,1:T(8,128)(2,1)} %copy.9), calls=%async_computation | async-start | bytes 8388608 | tf_op jit(solution)/shard_map/all_to_all | solution.py:15
  81.9 17.3 %all-gather.8.cloned.1.call-done = bf16[512,1664]{1,0:T(8,128)(2,1)} async-done(((bf16[256,1664]{1,0:T(8,128)(2,1)}), bf16[512,1664]{1,0:T(8,128)(2,1)}) %all-gather.8.cloned.1.call-update) | async-done | bytes 1703952 | tf_op jit(solution)/shard_map/all_gather | solution.py:16
  99.2 44.3 %all-to-all-done = bf16[256,2,4096]{2,0,1:T(8,128)(2,1)} async-done(((bf16[256,2,4096]{2,0,1:T(8,128)(2,1)}), bf16[256,2,4096]{2,0,1:T(8,128)(2,1)}, u32[]{:S(2)}, u32[]{:S(2)}) %all-to-all-start) | async-done | bytes 4194336 | tf_op jit(solution)/shard_map/all_to_all | solution.py:15
  143.5 18.2 %convert_reduce_fusion = bf16[1664,4096]{1,0:T(8,128)(2,1)} fusion(bf16[2,256,1664]{2,1,0:T(8,128)(2,1)} %bitcast.9, bf16[256,2,4096]{2,0,1:T(8,128)(2,1)} %all-to-all-done), kind=kOutput, calls=%fused_computation | convolution fusion | flops 6999769088 | bytes 19529728 | tf_op jit(solution)/shard_map/gtf,gtd->gfd/dot_general | solution.py:20
  161.7 267.6 %all-gather.6.cloned.1.call-done = bf16[1664,8192]{1,0:T(8,128)(2,1)} async-done(((bf16[1664,4096]{1,0:T(8,128)(2,1)}), bf16[1664,8192]{1,0:T(8,128)(2,1)}) %all-gather.6.cloned.1.call-update) | async-done | bytes 27262992 | tf_op jit(solution)/shard_map/all_gather | solution.py:8
  429.3 14.9 %convolution_convert_fusion = bf16[256,1664]{1,0:T(8,128)(2,1)} fusion(bf16[256,8192]{1,0:T(8,128)(2,1)} %all-gather.4.cloned.1.call-done, bf16[1664,8192]{1,0:T(8,128)(2,1)} %all-gather.6.cloned.1.call-done), kind=kOutput, calls=%fused_computation.2 | convolution fusion | flops 6979747840 | bytes 32309248 | tf_op jit(solution)/shard_map/dot_general | solution.py:12
Async XLA Ops:
  7.2 56.3 %all-gather.4.cloned.1.call-start = ((), (), s32[]{:S(2)}) async-start(), calls=%async_computation.1 | async-start | bytes 4456448 | tf_op jit(solution)/shard_map/all_gather | solution.py:11
  7.9 91.3 %all-gather.8.cloned.1.call-start = ((), (), s32[]{:S(2)}) async-start(), calls=%async_computation.3 | async-start | bytes 2555904 | tf_op jit(solution)/shard_map/all_gather | solution.py:16
  8.6 420.6 %all-gather.6.cloned.1.call-start = ((), (), s32[]{:S(2)}) async-start(), calls=%async_computation.2 | async-start | bytes 40894464 | tf_op jit(solution)/shard_map/all_gather | solution.py:8
  76.3 67.2 %all-to-all-start = ((bf16[256,2,4096]{2,0,1:T(8,128)(2,1)}), bf16[256,2,4096]{2,0,1:T(8,128)(2,1)}, u32[]{:S(2)}, u32[]{:S(2)}) async-start(bf16[256,2,4096]{2,0,1:T(8,128)(2,1)} %copy.9), calls=%async_computation | async-start | bytes 8388608 | tf_op jit(solution)/shard_map/all_to_all | solution.py:15
Sparse Core Ops, SparseCore 0:
  10.2 53.2 all-gather.3
  65.0 34.1 all-gather.7
  100.8 328.4 all-gather.5
where the time goes:
time: 451 us
  waiting for transfers between devices  385 us (85%)
  matrix products  33.1 us (7%)
  between operations  13.8 us (3%)
  local copies, waits for them, and re-layouts  12.9 us (3%)
  starting transfers between devices  5.67 us (1%)
    all_gather x1, waiting for transfers between devices, shards(): whole_weight = lax.all_gather(down_weight, 'dp', axis=1, tiled=True)  268 us
    all_gather x1, waiting for transfers between devices, shards(): received = lax.all_gather(out_grad, 'tp', axis=0, tiled=True)  54.1 us
    all_to_all x1, waiting for transfers between devices, shards(): lax.all_to_all(received, 'dp', split_axis=1, concat_axis=0, tiled=True)  44.3 us
    dot_general x1, matrix products, shards(): jnp.einsum('gtf,gtd->gfd', hidden_groups, grad_groups, preferred_element_...  18.2 us
    all_gather x1, waiting for transfers between devices, shards(): hidden_all = lax.all_gather(hidden, 'dp', axis=0, tiled=True)  17.3 us
    dot_general x1, matrix products, shards(): lax.dot_general(received, whole_weight, (((1,), (1,)), ((), ())), preferr...  14.9 us
  transfers between devices with their start and end apart: 4, of which 4 were waited for; matrix products, arithmetic and copies ran while one was open for 7% of the time, Pallas kernels for 0%

commit v1 on v0

v1 whole, which is shorter than its diff:
```python
import jax
import jax.numpy as jnp
from jax import lax
from jax.sharding import PartitionSpec as P


def shards(hidden, out_grad, down_weight):
    own = lax.all_to_all(out_grad, "dp", split_axis=1, concat_axis=0, tiled=True)
    dp = lax.axis_size("dp")
    own = own.reshape(dp, out_grad.shape[0], own.shape[1])
    grads = lax.all_gather(own, "tp", axis=1, tiled=True)
    grads = grads.reshape(-1, grads.shape[2])
    hidden_all = lax.all_gather(hidden, "dp", axis=0, tiled=True)
    partial = lax.dot_general(
        grads, down_weight, (((1,), (1,)), ((), ())), preferred_element_type=jnp.float32
    )
    input_grad = lax.psum_scatter(partial, "dp", scatter_dimension=0, tiled=True)
    weight_grad = lax.dot_general(
        hidden_all, grads, (((0,), (0,)), ((), ())), preferred_element_type=jnp.float32
    )
    return (input_grad.astype(jnp.bfloat16), weight_grad.astype(jnp.bfloat16))


def solution(mesh):
    placed = (P("dp", "tp"), P(("dp", "tp"), None), P("tp", "dp"))
    return jax.shard_map(
        shards,
        mesh=mesh,
        in_specs=placed,
        out_specs=(P("dp", "tp"), P("tp", "dp")),
        check_vma=False,
    )
```

time: 451 us -> 156 us (0.35)
  waiting for transfers between devices: 385 us -> 95.7 us
  blocking collectives: 0 us -> 9.18 us
  matrix products: 33.1 us -> 25.6 us
  starting transfers between devices: 5.67 us -> 0.12 us
    all_gather x2 -> x1, waiting for transfers between devices: 322 us -> 50.3 us  [shards(): grads = lax.all_gather(own, 'tp', axis=1, tiled=True)]
    all_to_all x1 -> x0, waiting for transfers between devices: 44.3 us -> none  [shards(): lax.all_to_all(received, 'dp', split_axis=1, concat_axis=0, tiled=True)]
    reduce_scatter x0 -> x1, waiting for transfers between devices: none -> 36 us  [shards(): lax.psum_scatter(partial, 'dp', scatter_dimension=0, tiled=True)]
    all_to_all x0 -> x1, blocking collectives: none -> 9.18 us  [shards(): lax.all_to_all(out_grad, 'dp', split_axis=1, concat_axis=0, tiled=True)]
    all_gather x1, waiting for transfers between devices: 17.3 us -> 8.6 us  [shards(): hidden_all = lax.all_gather(hidden, 'dp', axis=0, tiled=True)]
    dot_general x2, matrix products: 33.1 us -> 25.6 us  [the longest x1 13.1 us: shards(): lax.dot_general(grads, down_weight, (((1,), (1,)), ((), ())), preferred_e...]
    all_to_all x1 -> x0, starting transfers between devices: 5.56 us -> none  [shards(): lax.all_to_all(received, 'dp', split_axis=1, concat_axis=0, tiled=True)]
    all_to_all x1 -> x2, local copies, waits for them, and re-layouts: 6.52 us -> 1.94 us  [shards(): lax.all_to_all(out_grad, 'dp', split_axis=1, concat_axis=0, tiled=True)]
  transfers between devices with their start and end apart: 4 -> 3, of which waited for: 4 -> 3; matrix products, arithmetic and copies ran while one was open for 7% -> 20% of each run, Pallas kernels for 0% -> 0%
where the time goes in v1:
time: 156 us
  waiting for transfers between devices  95.7 us (61%)
  matrix products  25.6 us (16%)
  between operations  13.8 us (9%)
  blocking collectives  9.18 us (6%)
  local copies, waits for them, and re-layouts  8.97 us (6%)
  other arithmetic  2.44 us (2%)
    all_gather x1, waiting for transfers between devices, shards(): grads = lax.all_gather(own, 'tp', axis=1, tiled=True)  50.3 us
    reduce_scatter x1, waiting for transfers between devices, shards(): lax.psum_scatter(partial, 'dp', scatter_dimension=0, tiled=True)  36 us
    dot_general x1, matrix products, shards(): lax.dot_general(grads, down_weight, (((1,), (1,)), ((), ())), preferred_e...  13.1 us
    dot_general x1, matrix products, shards(): lax.dot_general(hidden_all, grads, (((0,), (0,)), ((), ())), preferred_el...  12.5 us
    all_to_all x1, blocking collectives, shards(): lax.all_to_all(out_grad, 'dp', split_axis=1, concat_axis=0, tiled=True)  9.18 us
    all_gather x1, waiting for transfers between devices, shards(): hidden_all = lax.all_gather(hidden, 'dp', axis=0, tiled=True)  8.6 us
    all_gather x1, local copies, waits for them, and re-layouts, shards(): grads = lax.all_gather(own, 'tp', axis=1, tiled=True)  5.1 us
  transfers between devices with their start and end apart: 3, of which 3 were waited for; matrix products, arithmetic and copies ran while one was open for 20% of the time, Pallas kernels for 0%

profile of v1, /device:TPU:0, one launch (start us, length us, event | category | flops | bytes accessed | tf_op | source)
XLA Modules:
  0.0 155.7 jit_solution(16338716906834858567)
XLA Ops:
  7.2 0.0 all-gather.3.cloned.1.call-start
  7.2 1.0 copy.11
  8.2 9.2 %all_to_all.16 = bf16[16,2,4096]{2,0,1:T(8,128)(2,1)S(1)} all-to-all(bf16[16,2,4096]{2,0,1:T(8,128)(2,1)S(1)} %bitcast.13), channel_id=1, replica_groups=mesh['dp'=2,'tp'=16] {'dp'}, dimensions={1} | all-to-all | bytes 524288 | tf_op jit(solution)/shard_map/all_to_all | solution.py:8
  17.4 1.0 copy.7
  18.3 0.0 all-gather.3.cloned.1.call-update
  18.4 0.0 all-gather.5.cloned.1.call-start
  18.4 0.7 all-gather.5.cloned.1.call-update
  19.1 0.0 reduce-scatter.2.cloned.1.call-start
  19.2 50.3 %all-gather.3.cloned.1.call-done = bf16[2,256,4096]{2,0,1:T(2,128)(2,1)} async-done(((bf16[2,16,4096]{2,0,1:T(2,128)(2,1)}), bf16[2,256,4096]{2,0,1:T(2,128)(2,1)}) %all-gather.3.cloned.1.call-update) | async-done | bytes 4194320 | tf_op jit(solution)/shard_map/all_gather | solution.py:11
  69.5 5.1 %copy.8 = bf16[2,256,4096]{2,1,0:T(8,128)(2,1)S(1)} copy(bf16[2,256,4096]{2,0,1:T(2,128)(2,1)} %all-gather.3.cloned.1.call-done) | data formatting | bytes 8388608 | tf_op jit(solution)/shard_map/all_gather | solution.py:11
  74.6 0.0 copy-start
  74.6 1.9 %copy-done = bf16[2,256,4096]{2,1,0:T(8,128)(2,1)} copy-done((bf16[2,256,4096]{2,1,0:T(8,128)(2,1)}, bf16[2,256,4096]{2,1,0:T(8,128)(2,1)S(1)}, u32[]{:S(2)}) %copy-start) | copy-done | bytes 4194328
  76.5 13.1 %fusion = f32[512,1664]{1,0:T(8,128)} fusion(bf16[512,4096]{1,0:T(8,128)(2,1)S(1)} %bitcast.10, bf16[1664,4096]{1,0:T(8,128)(2,1)} %param.5), kind=kOutput, calls=%fused_computation.2 | convolution fusion | flops 6979321856 | bytes 21233664 | tf_op jit(solution)/shard_map/dot_general | solution.py:14
  89.6 0.0 reduce-scatter.2.cloned.1.call-update
  89.6 8.6 %all-gather.5.cloned.1.call-done = bf16[512,1664]{1,0:T(8,128)(2,1)} async-done(((bf16[256,1664]{1,0:T(8,128)(2,1)}), bf16[512,1664]{1,0:T(8,128)(2,1)}) %all-gather.5.cloned.1.call-update) | async-done | bytes 1703952 | tf_op jit(solution)/shard_map/all_gather | solution.py:13
  98.3 12.5 %convolution_convert_fusion = bf16[1664,4096]{1,0:T(8,128)(2,1)} fusion(bf16[512,1664]{1,0:T(8,128)(2,1)} %all-gather.5.cloned.1.call-done, bf16[512,4096]{1,0:T(8,128)(2,1)} %bitcast.11), kind=kOutput, calls=%fused_computation | convolution fusion | flops 6986137600 | bytes 19529728 | tf_op jit(solution)/shard_map/dot_general | solution.py:18
  110.7 36.0 %reduce-scatter.2.cloned.1.call-done = f32[256,1664]{1,0:T(8,128)} async-done(((f32[512,1664]{1,0:T(8,128)}), f32[256,1664]{1,0:T(8,128)}) %reduce-scatter.2.cloned.1.call-update) | async-done | bytes 1703952 | tf_op jit(solution)/shard_map/reduce_scatter | solution.py:17
  146.7 2.4 %convert_element_type.6 = bf16[256,1664]{1,0:T(8,128)(2,1)} convert(f32[256,1664]{1,0:T(8,128)} %reduce-scatter.2.cloned.1.call-done) | non-fusion elementwise | flops 425984 | bytes 2555904 | tf_op jit(solution)/shard_map/convert_element_type | solution.py:21
Async XLA Ops:
  7.2 62.3 %all-gather.3.cloned.1.call-start = ((), (), s32[]{:S(2)}) async-start(), calls=%async_computation.2 | async-start | bytes 4456448 | tf_op jit(solution)/shard_map/all_gather | solution.py:11
  18.4 79.9 %all-gather.5.cloned.1.call-start = ((), (), s32[]{:S(2)}) async-start(), calls=%async_computation.4 | async-start | bytes 2555904 | tf_op jit(solution)/shard_map/all_gather | solution.py:13
  19.1 127.6 %reduce-scatter.2.cloned.1.call-start = ((), (), s32[]{:S(2)}) async-start(), calls=%async_computation.3 | async-start | bytes 5111808 | tf_op jit(solution)/shard_map/reduce_scatter | solution.py:17
  74.6 1.9 %copy-start = (bf16[2,256,4096]{2,1,0:T(8,128)(2,1)}, bf16[2,256,4096]{2,1,0:T(8,128)(2,1)S(1)}, u32[]{:S(2)}) copy-start(bf16[2,256,4096]{2,1,0:T(8,128)(2,1)S(1)} %copy.8) | copy-start | bytes 12582916
Sparse Core Ops, SparseCore 0:
  18.5 50.9 all-gather.2
  71.0 27.1 all-gather.4
  100.5 46.2 reduce-scatter.1

commit v2 on v1

--- a/solution.py
+++ b/solution.py
@@ -1,10 +1,257 @@
+import functools
+
 import jax
 import jax.numpy as jnp
 from jax import lax
+from jax.experimental import pallas as pl
+from jax.experimental.pallas import tpu as pltpu
 from jax.sharding import PartitionSpec as P
 
+CORES = 2
+ROWS = 2
+WIDE = 256
+HID_PARTS = 4
+X, UP, DOWN, Y, CORE = range(5)
+
+
+def gather_kernel(tp, hid, og, w, grads, hid_all, part_other, part_own,
+                  og_s, w_s, pb_s, pf_s,
+                  send, recv, hsend, hrecv, local, wsem, gsem):
+    i = lax.axis_index("dp")
+    j = lax.axis_index("tp")
+    depth = tp // (CORES * ROWS)
+    c = lax.rem(j, CORES)
+    y = lax.rem(j // CORES, ROWS)
+    z = j // (CORES * ROWS)
+    other = 1 - i
+    tok = hid.shape[0]
+    units = w.shape[0]
+    half = w.shape[1]
+    rows = og.shape[0]
+
+    def index(zz, yy, cc):
+        return (zz * ROWS + yy) * CORES + cc
+
+    places = {
+        X: (other, j),
+        UP: (i, index(z + 1, y, c)),
+        DOWN: (i, index(z - 1, y, c)),
+        Y: (i, index(z, 1 - y, c)),
+        CORE: (i, index(z, y, 1 - c)),
+    }
+    has = {UP: z < depth - 1, DOWN: z > 0}
+
+    def guarded(way, f):
+        if way in has:
+            pl.when(has[way])(f)
+        else:
+            f()
+
+    starts = list(range(0, units, WIDE))
+    w_copies = []
+    for k, s in enumerate(starts):
+        n = min(WIDE, units - s)
+        w_copies.append(pltpu.make_async_copy(
+            w.at[pl.ds(s, n), :], w_s.at[pl.ds(s, n), :], wsem.at[k]))
+        w_copies[-1].start()
+    mine = pl.ds(pl.multiple_of(i * half, 128), half)
+    theirs = pl.ds(pl.multiple_of(other * half, 128), half)
+    own_og = pltpu.make_async_copy(og.at[:, mine], og_s.at[i, j], local.at[0])
+    own_og.start()
+    own_rows = pl.ds(pl.multiple_of(i * tok, 128), tok)
+    own_hid = pltpu.make_async_copy(hid, hid_all.at[own_rows, :], local.at[1])
+    own_hid.start()
+
+    barrier = pltpu.get_barrier_semaphore()
+    for way in (X, UP, DOWN, Y, CORE):
+        def greet(way=way):
+            pl.semaphore_signal(barrier, inc=1, device_id=places[way],
+                                device_id_type=pl.DeviceIdType.MESH)
+        guarded(way, greet)
+    pl.semaphore_wait(barrier, 3 + jnp.where(z < depth - 1, 1, 0) + jnp.where(z > 0, 1, 0))
+
+    cross = pltpu.make_async_remote_copy(
+        og.at[:, theirs], og_s.at[i, j], send.at[X, i, j], recv.at[i, j],
+        device_id=places[X], device_id_type=pl.DeviceIdType.MESH)
+    cross.start()
+    step = tok // HID_PARTS
+    hid_copies = []
+    for k in range(HID_PARTS):
+        at = pl.ds(pl.multiple_of(i * tok + k * step, 16), step)
+        hid_copies.append(pltpu.make_async_remote_copy(
+            hid.at[pl.ds(k * step, step), :], hid_all.at[at, :], hsend.at[k], hrecv.at[k],
+            device_id=places[X], device_id_type=pl.DeviceIdType.MESH))
+        hid_copies[-1].start()
+
+    def block_copy(way, g, t):
+        return pltpu.make_async_remote_copy(
+            og_s.at[g, t], og_s.at[g, t], send.at[way, g, t], recv.at[g, t],
+            device_id=places[way], device_id_type=pl.DeviceIdType.MESH)
+
+    def keep(g, t):
+        rows_at = pl.ds(pl.multiple_of((g * tp + t) * rows, 16), rows)
+        return pltpu.make_async_copy(og_s.at[g, t], grads.at[rows_at, :], gsem.at[g, t])
+
+    def arrived(g, t):
+        block_copy(CORE, g, t).wait_recv()
+
+    def pass_on(g, t, ways):
+        for way in ways:
+            guarded(way, lambda way=way: block_copy(way, g, t).start())
+        keep(g, t).start()
+
+    def hops(g):
+        def own():
+            pass_on(g, j, (UP, DOWN, Y, CORE))
+
+        def along(s):
+            def below():
+                t = index(z - s, y, c)
+                arrived(g, t)
+                pass_on(g, t, (UP, Y, CORE))
+
+            def above():
+                t = index(z + s, y, c)
+                arrived(g, t)
+                pass_on(g, t, (DOWN, Y, CORE))
+
+            pl.when(z - s >= 0)(below)
+            pl.when(z + s < depth)(above)
+
+        def across(s):
+            def one(zz):
+                t = index(zz, 1 - y, c)
+                arrived(g, t)
+                pass_on(g, t, (CORE,))
+
+            if s == 0:
+                one(z)
+            else:
+                pl.when(z - s >= 0)(lambda: one(z - s))
+                pl.when(z + s < depth)(lambda: one(z + s))
+
+        steps = [own]
+        for s in range(1, depth):
+            steps.append(functools.partial(along, s))
+            steps.append(functools.partial(across, s - 1))
+        steps.append(functools.partial(across, depth - 1))
+        return steps
+
+    def from_core(g):
+        @pl.loop(0, depth * ROWS)
+        def _(k):
+            t = k * CORES + 1 - c
+            arrived(g, t)
+            keep(g, t).start()
+
+    def multiply(g, k, store):
+        s = starts[k]
+        n = min(WIDE, units - s)
+        if waited[k] == 0:
+            w_copies[k].wait()
+            waited[k] = 1
+        lhs = og_s[g].reshape(tp * rows, half)
+        store(s, n, lax.dot_general(lhs, w_s[pl.ds(s, n), :], (((1,), (1,)), ((), ())),
+                                    preferred_element_type=jnp.float32))
+
+    waited = [0] * len(starts)
+    own_og.wait()
+    own_steps = hops(i)
+    own_steps[0]()
+    arrived(other, j)
+    for f in hops(other):
+        f()
+    from_core(other)
+
+    def store_other(s, n, v):
+        pb_s[:, pl.ds(s, n)] = v.astype(jnp.bfloat16)
+
+    def store_own(s, n, v):
+        pf_s[:, pl.ds(s, n)] = v
+
+    rest = own_steps[1:]
+    for k in range(max(len(starts), len(rest))):
+        if k < len(starts):
+            multiply(other, k, store_other)
+        if k < len(rest):
+            rest[k]()
+    out_other = pltpu.make_async_copy(pb_s, part_other, local.at[2])
+    out_other.start()
+    from_core(i)
+    for k in range(len(starts)):
+        multiply(i, k, store_own)
+    out_own = pltpu.make_async_copy(pf_s, part_own, local.at[3])
+    out_own.start()
+
+    cross.wait_send()
+    for copy in hid_copies:
+        copy.wait()
+
+    @pl.loop(0, CORES * depth * ROWS)
+    def _(t):
+        for g in range(2):
+            keep(g, t).wait()
+    for g in (0, 1):
+        @pl.loop(0, depth)
+        def _(zz, g=g):
+            t = index(zz, y, c)
+            pl.when((zz <= z) & (z < depth - 1))(lambda: block_copy(UP, g, t).wait_send())
+            pl.when((zz >= z) & (z > 0))(lambda: block_copy(DOWN, g, t).wait_send())
+            block_copy(Y, g, t).wait_send()
+            block_copy(CORE, g, t).wait_send()
+            block_copy(CORE, g, index(zz, 1 - y, c)).wait_send()
+    own_hid.wait()
+    out_other.wait()
+    out_own.wait()
+
+
+def gather(hidden, out_grad, down_weight, tp):
+    tok, units = hidden.shape
+    half = down_weight.shape[1]
+    rows = out_grad.shape[0]
+    dma = pltpu.SemaphoreType.DMA
+    anyspace = pl.BlockSpec(memory_space=pl.ANY)
+    return pl.pallas_call(
+        functools.partial(gather_kernel, tp),
+        out_shape=(
+            jax.ShapeDtypeStruct((2 * tok, half), jnp.bfloat16),
+            jax.ShapeDtypeStruct((2 * tok, units), jnp.bfloat16),
+            jax.ShapeDtypeStruct((tok, units), jnp.bfloat16),
+            jax.ShapeDtypeStruct((tok, units), jnp.float32),
+        ),
+        in_specs=[anyspace] * 3,
+        out_specs=[anyspace] * 4,
+        scratch_shapes=[
+            pltpu.VMEM((2, tp, rows, half), jnp.bfloat16),
+            pltpu.VMEM((units, half), jnp.bfloat16),
+            pltpu.VMEM((tok, units), jnp.bfloat16),
+            pltpu.VMEM((tok, units), jnp.float32),
+            dma((5, 2, tp)),
+            dma((2, tp)),
+            dma((HID_PARTS,)),
+            dma((HID_PARTS,)),
+            dma((4,)),
+            dma((pl.cdiv(units, WIDE),)),
+            dma((2, tp)),
+        ],
+        compiler_params=pltpu.CompilerParams(
+            collective_id=0, has_side_effects=True, vmem_limit_bytes=48 * 2**20),
+    )(hidden, out_grad, down_weight)
+
 
 def shards(hidden, out_grad, down_weight):
+    dp = lax.axis_size("dp")
+    tp = lax.axis_size("tp")
+    grads, hidden_all, part_other, part_own = gather(hidden, out_grad, down_weight, tp)
+    received = lax.ppermute(part_other, "dp", [(k, 1 - k) for k in range(dp)])
+    weight_grad = lax.dot_general(
+        hidden_all, grads, (((0,), (0,)), ((), ())), preferred_element_type=jnp.float32
+    ).astype(jnp.bfloat16)
+    input_grad = (part_own + received.astype(jnp.float32)).astype(jnp.bfloat16)
+    return (input_grad, weight_grad)
+
+
+def plain_shards(hidden, out_grad, down_weight):
     own = lax.all_to_all(out_grad, "dp", split_axis=1, concat_axis=0, tiled=True)
     dp = lax.axis_size("dp")
     own = own.reshape(dp, out_grad.shape[0], own.shape[1])
@@ -21,10 +268,22 @@
     return (input_grad.astype(jnp.bfloat16), weight_grad.astype(jnp.bfloat16))
 
 
+def choose(dp, tp, hidden, out_grad, down_weight):
+    def run(hidden, out_grad, down_weight):
+        rows = out_grad.shape[0]
+        fits = (
+            dp == 2 and tp % (CORES * ROWS) == 0 and rows % 16 == 0
+            and hidden.shape[0] % (16 * HID_PARTS) == 0
+            and hidden.shape[1] % 128 == 0 and down_weight.shape[1] % 128 == 0
+        )
+        return (shards if fits else plain_shards)(hidden, out_grad, down_weight)
+    return run(hidden, out_grad, down_weight)
+
+
 def solution(mesh):
     placed = (P("dp", "tp"), P(("dp", "tp"), None), P("tp", "dp"))
     return jax.shard_map(
-        shards,
+        functools.partial(choose, mesh.shape["dp"], mesh.shape["tp"]),
         mesh=mesh,
         in_specs=placed,
         out_specs=(P("dp", "tp"), P("tp", "dp")),

time: 156 us -> 73.6 us (0.47)
  waiting for transfers between devices: 95.7 us -> 7.72 us
  Pallas kernels: 0 us -> 48.2 us
  between operations: 13.8 us -> 0.65 us
  matrix products: 25.6 us -> 13 us
  blocking collectives: 9.18 us -> 0 us
  local copies, waits for them, and re-layouts: 8.97 us -> 2.1 us
    all_gather x2 -> x0, waiting for transfers between devices: 58.9 us -> none  [the longest x1 50.3 us: shards(): grads = lax.all_gather(own, 'tp', axis=1, tiled=True)]
    pallas_call x0 -> x1, Pallas kernels: none -> 48.2 us  [gather(): pl.pallas_call(functools.partial(gather_kernel, tp), out_shape=(jax.Shape...]
    reduce_scatter x1 -> x0, waiting for transfers between devices: 36 us -> none  [shards(): lax.psum_scatter(partial, 'dp', scatter_dimension=0, tiled=True)]
    dot_general x1 -> x0, matrix products: 13.1 us -> none  [shards(): lax.dot_general(grads, down_weight, (((1,), (1,)), ((), ())), preferred_e...]
    all_to_all x1 -> x0, blocking collectives: 9.18 us -> none  [shards(): lax.all_to_all(out_grad, 'dp', split_axis=1, concat_axis=0, tiled=True)]
    ppermute x0 -> x1, waiting for transfers between devices: none -> 7.72 us  [shards(): received = lax.ppermute(part_other, 'dp', [(k, 1 - k) for k in range(dp)])]
    all_gather x1 -> x0, local copies, waits for them, and re-layouts: 5.1 us -> none  [shards(): grads = lax.all_gather(own, 'tp', axis=1, tiled=True)]
    all_to_all x2 -> x0, local copies, waits for them, and re-layouts: 1.94 us -> none  [shards(): lax.all_to_all(out_grad, 'dp', split_axis=1, concat_axis=0, tiled=True)]
  transfers between devices with their start and end apart: 3 -> 1, of which waited for: 3 -> 1; matrix products, arithmetic and copies ran while one was open for 20% -> 18% of each run, Pallas kernels for 0% -> 0%
where the time goes in v2:
time: 73.6 us; the launch traced here: 73.4 us
  Pallas kernels  48.2 us (65%)
  matrix products  13 us (18%)
  waiting for transfers between devices  7.72 us (10%)
  local copies, waits for them, and re-layouts  2.1 us (3%)
  other arithmetic  1.08 us (1%)
    pallas_call x1, Pallas kernels, gather(): pl.pallas_call(functools.partial(gather_kernel, tp), out_shape=(jax.Shape...  48.2 us
    dot_general x1, matrix products, shards(): lax.dot_general(hidden_all, grads, (((0,), (0,)), ((), ())), preferred_el...  13 us
    ppermute x1, waiting for transfers between devices, shards(): received = lax.ppermute(part_other, 'dp', [(k, 1 - k) for k in range(dp)])  7.72 us
    unnamed x4, local copies, waits for them, and re-layouts  2.1 us
  transfers between devices with their start and end apart: 1, of which 1 were waited for; matrix products, arithmetic and copies ran while one was open for 18% of the time, Pallas kernels for 0%

profile of v2, /device:TPU:0, one launch (start us, length us, event | category | flops | bytes accessed | tf_op | source)
XLA Modules:
  0.0 73.4 jit_solution(1053165249013017884)
XLA Ops:
  0.6 0.0 copy-start
  0.6 1.1 %copy-done = bf16[256,1664]{1,0:T(8,128)(2,1)S(1)} copy-done((bf16[256,1664]{1,0:T(8,128)(2,1)S(1)}, bf16[256,1664]{1,0:T(8,128)(2,1)}, u32[]{:S(2)}) %copy-start) | copy-done | bytes 851992
  1.8 0.0 copy-start.1
  1.8 0.9 %copy-done.1 = bf16[16,8192]{1,0:T(8,128)(2,1)S(1)} copy-done((bf16[16,8192]{1,0:T(8,128)(2,1)S(1)}, bf16[16,8192]{1,0:T(8,128)(2,1)}, u32[]{:S(2)}) %copy-start.1) | copy-done | bytes 262168
  2.7 48.2 %shard_map.50 = (bf16[512,4096]{1,0:T(8,128)(2,1)}, bf16[512,1664]{1,0:T(8,128)(2,1)S(1)}, bf16[256,1664]{1,0:T(8,128)(2,1)S(1)}, f32[256,1664]{1,0:T(8,128)S(1)}) custom-call(bf16[256,1664]{1,0:T(8,128)(2,1)S(1)} %copy-done, bf16[16,8192]{1,0:T(8,128)(2,1)S(1)} %copy-done.1, bf16[1664,4096]{1,0:T(8,128)(2,1)} %w.1), custom_call_target="tpu_custom_call" | custom-call | tf_op jit(solution)/shard_map/pallas_call | solution.py:214
  51.0 0.6 collective-permute-start
  51.6 13.0 %convolution_convert_fusion = bf16[1664,4096]{1,0:T(8,128)(2,1)} fusion(bf16[512,1664]{1,0:T(8,128)(2,1)S(1)} %get-tuple-element.8, bf16[512,4096]{1,0:T(8,128)(2,1)} %get-tuple-element.9), kind=kOutput, calls=%fused_computation | convolution fusion | flops 6986137600 | bytes 19529728 | tf_op jit(solution)/shard_map/dot_general | solution.py:247
  64.6 7.7 %collective-permute-done = bf16[256,1664]{1,0:T(8,128)(2,1)S(1)} collective-permute-done((bf16[256,1664]{1,0:T(8,128)(2,1)S(1)}, bf16[256,1664]{1,0:T(8,128)(2,1)S(1)}, u32[]{:S(2)}, u32[]{:S(2)}) %collective-permute-start) | collective-permute-done | bytes 852000 | tf_op jit(solution)/shard_map/ppermute | solution.py:246
  72.3 1.1 %add_convert_fusion = bf16[256,1664]{1,0:T(8,128)(2,1)} fusion(f32[256,1664]{1,0:T(8,128)S(1)} %get-tuple-element.6, bf16[256,1664]{1,0:T(8,128)(2,1)S(1)} %collective-permute-done), kind=kLoop, calls=%fused_computation.1 | loop fusion | flops 1277952 | bytes 3407872 | tf_op jit(solution)/shard_map/convert_element_type | solution.py:250
Async XLA Ops:
  0.6 1.2 %copy-start = (bf16[256,1664]{1,0:T(8,128)(2,1)S(1)}, bf16[256,1664]{1,0:T(8,128)(2,1)}, u32[]{:S(2)}) copy-start(bf16[256,1664]{1,0:T(8,128)(2,1)} %hid.1) | copy-start | bytes 2555908
  1.8 0.9 %copy-start.1 = (bf16[16,8192]{1,0:T(8,128)(2,1)S(1)}, bf16[16,8192]{1,0:T(8,128)(2,1)}, u32[]{:S(2)}) copy-start(bf16[16,8192]{1,0:T(8,128)(2,1)} %og.1) | copy-start | bytes 786436
  51.0 21.3 %collective-permute-start = (bf16[256,1664]{1,0:T(8,128)(2,1)S(1)}, bf16[256,1664]{1,0:T(8,128)(2,1)S(1)}, u32[]{:S(2)}, u32[]{:S(2)}) collective-permute-start(bf16[256,1664]{1,0:T(8,128)(2,1)S(1)} %get-tuple-element.7), channel_id=1, source_target_pairs={{0,16},{16,0},{1,17},{17,1},{2,18},{18,2},{3,19},{19,3},{4,20},{20... | collective-permute-start | bytes 2555912 | tf_op jit(solution)/shard_map/ppermute | solution.py:246

commit v3 on v2

--- a/solution.py
+++ b/solution.py
@@ -11,12 +11,16 @@
 ROWS = 2
 WIDE = 256
 HID_PARTS = 4
+SENT = 3
+LEAD = 3
+LAG = 2
+TILE = 512
 X, UP, DOWN, Y, CORE = range(5)
 
 
-def gather_kernel(tp, hid, og, w, grads, hid_all, part_other, part_own,
+def gather_kernel(tp, sent, hid, og, w, grads, hid_all, part_other, part_here, part_own,
                   og_s, w_s, pb_s, pf_s,
-                  send, recv, hsend, hrecv, local, wsem, gsem):
+                  send, recv, hsend, hrecv, psend, precv, local, wsem, gsem):
     i = lax.axis_index("dp")
     j = lax.axis_index("tp")
     depth = tp // (CORES * ROWS)
@@ -159,8 +163,16 @@
     own_steps = hops(i)
     own_steps[0]()
     arrived(other, j)
-    for f in hops(other):
-        f()
+    other_steps = hops(other)
+    other_steps[0]()
+    count = len(own_steps)
+    for k in range(1, LEAD):
+        own_steps[k]()
+        other_steps[k]()
+    for k in range(LEAD, count):
+        other_steps[k]()
+        if k < count - LAG:
+            own_steps[k]()
     from_core(other)
 
     def store_other(s, n, v):
@@ -169,13 +181,21 @@
     def store_own(s, n, v):
         pf_s[:, pl.ds(s, n)] = v
 
-    rest = own_steps[1:]
+    rest = own_steps[max(LEAD, count - LAG):]
+    swaps = []
     for k in range(max(len(starts), len(rest))):
         if k < len(starts):
             multiply(other, k, store_other)
+            if k < sent:
+                cols = pl.ds(k * WIDE, WIDE)
+                swaps.append(pltpu.make_async_remote_copy(
+                    pb_s.at[:, cols], part_here.at[:, cols], psend.at[k], precv.at[k],
+                    device_id=places[X], device_id_type=pl.DeviceIdType.MESH))
+                swaps[-1].start()
         if k < len(rest):
             rest[k]()
-    out_other = pltpu.make_async_copy(pb_s, part_other, local.at[2])
+    out_other = pltpu.make_async_copy(
+        pb_s.at[:, pl.ds(sent * WIDE, units - sent * WIDE)], part_other, local.at[2])
     out_other.start()
     from_core(i)
     for k in range(len(starts)):
@@ -184,7 +204,7 @@
     out_own.start()
 
     cross.wait_send()
-    for copy in hid_copies:
+    for copy in hid_copies + swaps:
         copy.wait()
 
     @pl.loop(0, CORES * depth * ROWS)
@@ -210,17 +230,19 @@
     half = down_weight.shape[1]
     rows = out_grad.shape[0]
     dma = pltpu.SemaphoreType.DMA
+    sent = max(1, units // WIDE * SENT // 6)
     anyspace = pl.BlockSpec(memory_space=pl.ANY)
     return pl.pallas_call(
-        functools.partial(gather_kernel, tp),
+        functools.partial(gather_kernel, tp, sent),
         out_shape=(
             jax.ShapeDtypeStruct((2 * tok, half), jnp.bfloat16),
             jax.ShapeDtypeStruct((2 * tok, units), jnp.bfloat16),
-            jax.ShapeDtypeStruct((tok, units), jnp.bfloat16),
+            jax.ShapeDtypeStruct((tok, units - sent * WIDE), jnp.bfloat16),
+            jax.ShapeDtypeStruct((tok, sent * WIDE), jnp.bfloat16),
             jax.ShapeDtypeStruct((tok, units), jnp.float32),
         ),
         in_specs=[anyspace] * 3,
-        out_specs=[anyspace] * 4,
+        out_specs=[anyspace] * 5,
         scratch_shapes=[
             pltpu.VMEM((2, tp, rows, half), jnp.bfloat16),
             pltpu.VMEM((units, half), jnp.bfloat16),
@@ -230,23 +252,55 @@
             dma((2, tp)),
             dma((HID_PARTS,)),
             dma((HID_PARTS,)),
+            dma((sent,)),
+            dma((sent,)),
             dma((4,)),
             dma((pl.cdiv(units, WIDE),)),
             dma((2, tp)),
         ],
         compiler_params=pltpu.CompilerParams(
-            collective_id=0, has_side_effects=True, vmem_limit_bytes=48 * 2**20),
+            collective_id=0, has_side_effects=True, vmem_limit_bytes=60 * 2**20),
     )(hidden, out_grad, down_weight)
+
+
+def weight_kernel(h, g, out, ht):
+    @pl.when(pl.program_id(0) == 0)
+    def _():
+        ht[...] = h[...].T
+
+    out[...] = jnp.dot(ht[...], g[...], preferred_element_type=jnp.float32).astype(out.dtype)
+
+
+def weight_gradient(hidden_all, grads):
+    tokens, units = hidden_all.shape
+    half = grads.shape[1]
+    tile = TILE if half % TILE == 0 else 128
+    return pl.pallas_call(
+        weight_kernel,
+        grid=(half // tile,),
+        out_shape=jax.ShapeDtypeStruct((units, half), jnp.bfloat16),
+        in_specs=[
+            pl.BlockSpec((tokens, units), lambda n: (0, 0)),
+            pl.BlockSpec((tokens, tile), lambda n: (0, n)),
+        ],
+        out_specs=pl.BlockSpec((units, tile), lambda n: (0, n)),
+        scratch_shapes=[pltpu.VMEM((units, tokens), jnp.bfloat16)],
+        compiler_params=pltpu.CompilerParams(vmem_limit_bytes=56 * 2**20),
+        cost_estimate=pl.CostEstimate(
+            flops=2 * tokens * units * half,
+            bytes_accessed=2 * (tokens * (units + half) + units * half),
+            transcendentals=0),
+    )(hidden_all, grads)
 
 
 def shards(hidden, out_grad, down_weight):
     dp = lax.axis_size("dp")
     tp = lax.axis_size("tp")
-    grads, hidden_all, part_other, part_own = gather(hidden, out_grad, down_weight, tp)
+    grads, hidden_all, part_other, part_here, part_own = gather(
+        hidden, out_grad, down_weight, tp)
     received = lax.ppermute(part_other, "dp", [(k, 1 - k) for k in range(dp)])
-    weight_grad = lax.dot_general(
-        hidden_all, grads, (((0,), (0,)), ((), ())), preferred_element_type=jnp.float32
-    ).astype(jnp.bfloat16)
+    weight_grad = weight_gradient(hidden_all, grads)
+    received = jnp.concatenate([part_here, received], axis=1)
     input_grad = (part_own + received.astype(jnp.float32)).astype(jnp.bfloat16)
     return (input_grad, weight_grad)
 

time: 73.6 us -> 65.4 us (0.89)
  matrix products: 13 us -> 0 us
  Pallas kernels: 48.2 us -> 61.1 us
  waiting for transfers between devices: 7.72 us -> 0.01 us
  local copies, waits for them, and re-layouts: 2.1 us -> 0.01 us
  starting transfers between devices: 0.63 us -> 1.68 us
    dot_general x1 -> x0, matrix products: 13 us -> none  [shards(): lax.dot_general(hidden_all, grads, (((0,), (0,)), ((), ())), preferred_el...]
    pallas_call x1 -> x2, Pallas kernels: 48.2 us -> 61.1 us  [the longest x1 47.9 us: gather(): pl.pallas_call(functools.partial(gather_kernel, tp, sent), out_shape=(jax...]
    ppermute x1, waiting for transfers between devices: 7.72 us -> 0.01 us  [shards(): received = lax.ppermute(part_other, 'dp', [(k, 1 - k) for k in range(dp)])]
    unnamed x4, local copies, waits for them, and re-layouts: 2.1 us -> 0.01 us
    ppermute x1, starting transfers between devices: 0.63 us -> 1.68 us  [shards(): received = lax.ppermute(part_other, 'dp', [(k, 1 - k) for k in range(dp)])]
  transfers between devices with their start and end apart: 1 -> 1, of which waited for: 1 -> 0; matrix products, arithmetic and copies ran while one was open for 18% -> 0% of each run, Pallas kernels for 0% -> 21%
where the time goes in v3:
time: 65.4 us; the launch traced here: 64.5 us
  Pallas kernels  61.1 us (93%)
  starting transfers between devices  1.68 us (3%)
  other arithmetic  1.04 us (2%)
    pallas_call x1, Pallas kernels, gather(): pl.pallas_call(functools.partial(gather_kernel, tp, sent), out_shape=(jax...  47.9 us
    pallas_call x1, Pallas kernels, weight_gradient(): pl.pallas_call(weight_kernel, grid=(half // tile,), out_shape=jax.ShapeDt...  13.2 us
    ppermute x1, starting transfers between devices, shards(): received = lax.ppermute(part_other, 'dp', [(k, 1 - k) for k in range(dp)])  1.68 us
  transfers between devices with their start and end apart: 1, of which 0 were waited for; matrix products, arithmetic and copies ran while one was open for 0% of the time, Pallas kernels for 21%

profile of v3, /device:TPU:0, one launch (start us, length us, event | category | flops | bytes accessed | tf_op | source)
XLA Modules:
  0.0 64.5 jit_solution(10694934184640267043)
XLA Ops:
  0.6 47.9 %shard_map.50 = (bf16[512,4096]{1,0:T(8,128)(2,1)}, bf16[512,1664]{1,0:T(8,128)(2,1)}, bf16[256,896]{1,0:T(8,128)(2,1)}, bf16[256,768]{1,0:T(8,128)(2,1)}, f32[256,1664]{1,0:T(8,128)}) custom-call(bf16[256,1664]{1,0:T(8,128)(2,1)} %hid.1, bf16[16,8192]{1,0:T(8,128)(2,1)} %og.1, bf16[1664,4096]{1,0:T(8,128)(2,1)} %w.1), custom_call_target="tpu_custom_call" | custom-call | tf_op jit(solution)/shard_map/pallas_call | solution.py:235
  48.5 1.7 %collective-permute-start = (bf16[256,896]{1,0:T(8,128)(2,1)}, bf16[256,896]{1,0:T(8,128)(2,1)S(1)}, u32[]{:S(2)}, u32[]{:S(2)}) collective-permute-start(bf16[256,896]{1,0:T(8,128)(2,1)} %get-tuple-element.9), channel_id=1, source_target_pairs={{0,16},{16,0},{1,17},{17,1},{2,18},{18,2},{3,19},{19,3},{4,20},{20... | collective-permute-start | bytes 1376264 | tf_op jit(solution)/shard_map/ppermute | solution.py:301
  50.2 0.0 copy-start
  50.2 0.0 copy-start.1
  50.2 13.2 %shard_map.51 = bf16[1664,4096]{1,0:T(8,128)(2,1)} custom-call(bf16[512,1664]{1,0:T(8,128)(2,1)} %get-tuple-element.10.h, bf16[512,4096]{1,0:T(8,128)(2,1)} %get-tuple-element.11.g), custom_call_target="tpu_custom_call" | custom-call | flops 6979321856 | bytes 19529728 | tf_op jit(solution)/shard_map/pallas_call | solution.py:278
  63.4 0.0 collective-permute-done
  63.4 0.0 copy-done
  63.4 0.0 copy-done.1
  63.4 1.0 %add_convert_fusion = bf16[256,1664]{1,0:T(8,128)(2,1)} fusion(f32[256,1664]{1,0:T(8,128)S(1)} %copy-done, bf16[256,896]{1,0:T(8,128)(2,1)S(1)} %collective-permute-done, bf16[256,768]{1,0:T(8,128)(2,1)S(1)} %copy-done.1), kind=kLoop, calls=%fused_computation | loop fusion | flops 2555904 | bytes 3407872 | tf_op jit(solution)/shard_map/convert_element_type | solution.py:304
Async XLA Ops:
  48.5 14.9 %collective-permute-start = (bf16[256,896]{1,0:T(8,128)(2,1)}, bf16[256,896]{1,0:T(8,128)(2,1)S(1)}, u32[]{:S(2)}, u32[]{:S(2)}) collective-permute-start(bf16[256,896]{1,0:T(8,128)(2,1)} %get-tuple-element.9), channel_id=1, source_target_pairs={{0,16},{16,0},{1,17},{17,1},{2,18},{18,2},{3,19},{19,3},{4,20},{20... | collective-permute-start | bytes 1376264 | tf_op jit(solution)/shard_map/ppermute | solution.py:301
  50.2 13.3 %copy-start = (f32[256,1664]{1,0:T(8,128)S(1)}, f32[256,1664]{1,0:T(8,128)}, u32[]{:S(2)}) copy-start(f32[256,1664]{1,0:T(8,128)} %get-tuple-element.7) | copy-start | bytes 5111812
  50.2 13.3 %copy-start.1 = (bf16[256,768]{1,0:T(8,128)(2,1)S(1)}, bf16[256,768]{1,0:T(8,128)(2,1)}, u32[]{:S(2)}) copy-start(bf16[256,768]{1,0:T(8,128)(2,1)} %get-tuple-element.8) | copy-start | bytes 1179652

commit v4 on v3

--- a/solution.py
+++ b/solution.py
@@ -11,15 +11,12 @@
 ROWS = 2
 WIDE = 256
 HID_PARTS = 4
-SENT = 3
-LEAD = 3
-LAG = 2
 TILE = 512
 X, UP, DOWN, Y, CORE = range(5)
 
 
-def gather_kernel(tp, sent, hid, og, w, grads, hid_all, part_other, part_here, part_own,
-                  og_s, w_s, pb_s, pf_s,
+def gather_kernel(tp, hid, og, w, grads, hid_all, part_other, part_here, part_own,
+                  og_s, w_s, pb_s,
                   send, recv, hsend, hrecv, psend, precv, local, wsem, gsem):
     i = lax.axis_index("dp")
     j = lax.axis_index("tp")
@@ -60,7 +57,7 @@
         w_copies[-1].start()
     mine = pl.ds(pl.multiple_of(i * half, 128), half)
     theirs = pl.ds(pl.multiple_of(other * half, 128), half)
-    own_og = pltpu.make_async_copy(og.at[:, mine], og_s.at[i, j], local.at[0])
+    own_og = pltpu.make_async_copy(og.at[:, mine], og_s.at[j, i], local.at[0])
     own_og.start()
     own_rows = pl.ds(pl.multiple_of(i * tok, 128), tok)
     own_hid = pltpu.make_async_copy(hid, hid_all.at[own_rows, :], local.at[1])
@@ -75,7 +72,7 @@
     pl.semaphore_wait(barrier, 3 + jnp.where(z < depth - 1, 1, 0) + jnp.where(z > 0, 1, 0))
 
     cross = pltpu.make_async_remote_copy(
-        og.at[:, theirs], og_s.at[i, j], send.at[X, i, j], recv.at[i, j],
+        og.at[:, theirs], og_s.at[j, i], send.at[X, i, j], recv.at[i, j],
         device_id=places[X], device_id_type=pl.DeviceIdType.MESH)
     cross.start()
     step = tok // HID_PARTS
@@ -89,12 +86,12 @@
 
     def block_copy(way, g, t):
         return pltpu.make_async_remote_copy(
-            og_s.at[g, t], og_s.at[g, t], send.at[way, g, t], recv.at[g, t],
+            og_s.at[t, g], og_s.at[t, g], send.at[way, g, t], recv.at[g, t],
             device_id=places[way], device_id_type=pl.DeviceIdType.MESH)
 
     def keep(g, t):
         rows_at = pl.ds(pl.multiple_of((g * tp + t) * rows, 16), rows)
-        return pltpu.make_async_copy(og_s.at[g, t], grads.at[rows_at, :], gsem.at[g, t])
+        return pltpu.make_async_copy(og_s.at[t, g], grads.at[rows_at, :], gsem.at[g, t])
 
     def arrived(g, t):
         block_copy(CORE, g, t).wait_recv()
@@ -141,66 +138,68 @@
         steps.append(functools.partial(across, depth - 1))
         return steps
 
-    def from_core(g):
-        @pl.loop(0, depth * ROWS)
+    near = z // (depth // 2)
+    run = tp // 2
+
+    def from_core(part):
+        first = part * (depth // 2) * ROWS
+
+        @pl.loop(0, depth // 2 * ROWS)
         def _(k):
-            t = k * CORES + 1 - c
-            arrived(g, t)
-            keep(g, t).start()
-
-    def multiply(g, k, store):
+            t = (first + k) * CORES + 1 - c
+            for g in range(2):
+                arrived(g, t)
+                keep(g, t).start()
+
+    def multiply(part, k):
         s = starts[k]
         n = min(WIDE, units - s)
         if waited[k] == 0:
             w_copies[k].wait()
             waited[k] = 1
-        lhs = og_s[g].reshape(tp * rows, half)
-        store(s, n, lax.dot_general(lhs, w_s[pl.ds(s, n), :], (((1,), (1,)), ((), ())),
-                                    preferred_element_type=jnp.float32))
+        at = pl.ds(part * run, run)
+        lhs = og_s[at].reshape(run * 2 * rows, half)
+        v = lax.dot_general(lhs, w_s[pl.ds(s, n), :], (((1,), (1,)), ((), ())),
+                            preferred_element_type=jnp.float32)
+        v = v.astype(jnp.bfloat16).reshape(run, 2, rows, n)
+        for g in range(2):
+            pb_s[g, at, :, pl.ds(s, n)] = v[:, g]
 
     waited = [0] * len(starts)
     own_og.wait()
     own_steps = hops(i)
+    other_steps = hops(other)
     own_steps[0]()
     arrived(other, j)
-    other_steps = hops(other)
     other_steps[0]()
-    count = len(own_steps)
-    for k in range(1, LEAD):
+    cut = depth // 2 * 2 + 1
+    for k in range(1, cut):
         own_steps[k]()
         other_steps[k]()
-    for k in range(LEAD, count):
-        other_steps[k]()
-        if k < count - LAG:
-            own_steps[k]()
-    from_core(other)
-
-    def store_other(s, n, v):
-        pb_s[:, pl.ds(s, n)] = v.astype(jnp.bfloat16)
-
-    def store_own(s, n, v):
-        pf_s[:, pl.ds(s, n)] = v
-
-    rest = own_steps[max(LEAD, count - LAG):]
+    from_core(near)
+    rest = []
+    for k in range(cut, len(own_steps)):
+        rest += [own_steps[k], other_steps[k]]
     swaps = []
     for k in range(max(len(starts), len(rest))):
-        if k < len(starts):
-            multiply(other, k, store_other)
-            if k < sent:
-                cols = pl.ds(k * WIDE, WIDE)
-                swaps.append(pltpu.make_async_remote_copy(
-                    pb_s.at[:, cols], part_here.at[:, cols], psend.at[k], precv.at[k],
-                    device_id=places[X], device_id_type=pl.DeviceIdType.MESH))
-                swaps[-1].start()
         if k < len(rest):
             rest[k]()
+        if k < len(starts):
+            multiply(near, k)
+            n = min(WIDE, units - starts[k])
+            cols = pl.ds(starts[k], n)
+            swaps.append(pltpu.make_async_remote_copy(
+                pb_s.at[other, pl.ds(near * run, run), :, cols], part_here.at[:, :, cols],
+                psend.at[k], precv.at[k],
+                device_id=places[X], device_id_type=pl.DeviceIdType.MESH))
+            swaps[-1].start()
+    from_core(1 - near)
+    for k in range(len(starts)):
+        multiply(1 - near, k)
     out_other = pltpu.make_async_copy(
-        pb_s.at[:, pl.ds(sent * WIDE, units - sent * WIDE)], part_other, local.at[2])
+        pb_s.at[other, pl.ds((1 - near) * run, run)], part_other, local.at[2])
     out_other.start()
-    from_core(i)
-    for k in range(len(starts)):
-        multiply(i, k, store_own)
-    out_own = pltpu.make_async_copy(pf_s, part_own, local.at[3])
+    out_own = pltpu.make_async_copy(pb_s.at[i], part_own, local.at[3])
     out_own.start()
 
     cross.wait_send()
@@ -230,30 +229,29 @@
     half = down_weight.shape[1]
     rows = out_grad.shape[0]
     dma = pltpu.SemaphoreType.DMA
-    sent = max(1, units // WIDE * SENT // 6)
+    pieces = pl.cdiv(units, WIDE)
     anyspace = pl.BlockSpec(memory_space=pl.ANY)
     return pl.pallas_call(
-        functools.partial(gather_kernel, tp, sent),
+        functools.partial(gather_kernel, tp),
         out_shape=(
             jax.ShapeDtypeStruct((2 * tok, half), jnp.bfloat16),
             jax.ShapeDtypeStruct((2 * tok, units), jnp.bfloat16),
-            jax.ShapeDtypeStruct((tok, units - sent * WIDE), jnp.bfloat16),
-            jax.ShapeDtypeStruct((tok, sent * WIDE), jnp.bfloat16),
-            jax.ShapeDtypeStruct((tok, units), jnp.float32),
+            jax.ShapeDtypeStruct((tp // 2, rows, units), jnp.bfloat16),
+            jax.ShapeDtypeStruct((tp // 2, rows, units), jnp.bfloat16),
+            jax.ShapeDtypeStruct((tp, rows, units), jnp.bfloat16),
         ),
         in_specs=[anyspace] * 3,
         out_specs=[anyspace] * 5,
         scratch_shapes=[
-            pltpu.VMEM((2, tp, rows, half), jnp.bfloat16),
+            pltpu.VMEM((tp, 2, rows, half), jnp.bfloat16),
             pltpu.VMEM((units, half), jnp.bfloat16),
-            pltpu.VMEM((tok, units), jnp.bfloat16),
-            pltpu.VMEM((tok, units), jnp.float32),
+            pltpu.VMEM((2, tp, rows, units), jnp.bfloat16),
             dma((5, 2, tp)),
             dma((2, tp)),
             dma((HID_PARTS,)),
             dma((HID_PARTS,)),
-            dma((sent,)),
-            dma((sent,)),
+            dma((pieces,)),
+            dma((pieces,)),
             dma((4,)),
             dma((pl.cdiv(units, WIDE),)),
             dma((2, tp)),
@@ -300,8 +298,11 @@
         hidden, out_grad, down_weight, tp)
     received = lax.ppermute(part_other, "dp", [(k, 1 - k) for k in range(dp)])
     weight_grad = weight_gradient(hidden_all, grads)
-    received = jnp.concatenate([part_here, received], axis=1)
-    input_grad = (part_own + received.astype(jnp.float32)).astype(jnp.bfloat16)
+    first = lax.axis_index("tp") < tp // 2
+    received = jnp.where(first, jnp.concatenate([part_here, received], axis=0),
+                         jnp.concatenate([received, part_here], axis=0))
+    input_grad = part_own.astype(jnp.float32) + received.astype(jnp.float32)
+    input_grad = input_grad.astype(jnp.bfloat16).reshape(hidden.shape)
     return (input_grad, weight_grad)
 
 
@@ -326,7 +327,7 @@
     def run(hidden, out_grad, down_weight):
         rows = out_grad.shape[0]
         fits = (
-            dp == 2 and tp % (CORES * ROWS) == 0 and rows % 16 == 0
+            dp == 2 and tp % (2 * CORES * ROWS) == 0 and rows % 16 == 0
             and hidden.shape[0] % (16 * HID_PARTS) == 0
             and hidden.shape[1] % 128 == 0 and down_weight.shape[1] % 128 == 0
         )

time: 65.4 us -> 59.7 us (0.913)
  the two profiles are of different devices: /device:TPU:0 before, /device:TPU:17 now
where the time goes in v4:
time: 59.7 us; the launch traced here: 59.4 us
  Pallas kernels  56.4 us (94%)
  starting transfers between devices  1.17 us (2%)
  other arithmetic  1.16 us (2%)
  between operations  0.64 us (1%)
    pallas_call x1, Pallas kernels, gather(): pl.pallas_call(functools.partial(gather_kernel, tp), out_shape=(jax.Shape...  43.2 us
    pallas_call x1, Pallas kernels, weight_gradient(): pl.pallas_call(weight_kernel, grid=(half // tile,), out_shape=jax.ShapeDt...  13.2 us
  transfers between devices with their start and end apart: 1, of which 0 were waited for; matrix products, arithmetic and copies ran while one was open for 0% of the time, Pallas kernels for 22%

profile of v4, /device:TPU:17, one launch (start us, length us, event | category | flops | bytes accessed | tf_op | source)
XLA Modules:
  0.0 59.4 jit_solution(16817755009016265223)
XLA Ops:
  0.6 43.2 %shard_map.50 = (bf16[512,4096]{1,0:T(8,128)(2,1)}, bf16[512,1664]{1,0:T(8,128)(2,1)}, bf16[8,16,1664]{2,1,0:T(8,128)(2,1)}, bf16[8,16,1664]{2,1,0:T(8,128)(2,1)}, bf16[16,16,1664]{2,1,0:T(8,128)(2,1)}) custom-call(bf16[256,1664]{1,0:T(8,128)(2,1)} %hid.1, bf16[16,8192]{1,0:T(8,128)(2,1)} %og.1, bf16[1664,4096]{1,0:T(8,128)(2,1)} %w.1), custom_call_target="tpu_custom_call" | custom-call | tf_op jit(solution)/shard_map/pallas_call | solution.py:234
  43.9 1.2 %collective-permute-start = (bf16[8,16,1664]{2,1,0:T(8,128)(2,1)}, bf16[8,16,1664]{2,1,0:T(8,128)(2,1)S(1)}, u32[]{:S(2)}, u32[]{:S(2)}) collective-permute-start(bf16[8,16,1664]{2,1,0:T(8,128)(2,1)} %get-tuple-element.9), channel_id=1, source_target_pairs={{0,16},{16,0},{1,17},{17,1},{2,18},{18,2},{3,19},{19,3},{4,20},{20... | collective-permute-start | bytes 1277960 | tf_op jit(solution)/shard_map/ppermute | solution.py:299
  45.0 0.0 copy-start
  45.0 0.0 copy-start.1
  45.0 13.2 %shard_map.51 = bf16[1664,4096]{1,0:T(8,128)(2,1)} custom-call(bf16[512,1664]{1,0:T(8,128)(2,1)} %get-tuple-element.10.h, bf16[512,4096]{1,0:T(8,128)(2,1)} %get-tuple-element.11.g), custom_call_target="tpu_custom_call" | custom-call | flops 6979321856 | bytes 19529728 | tf_op jit(solution)/shard_map/pallas_call | solution.py:276
  58.3 0.0 collective-permute-done
  58.3 0.0 copy-done
  58.3 0.0 copy-done.1
  58.3 1.2 %add_convert_fusion = bf16[16,16,1664]{2,1,0:T(8,128)(2,1)} fusion(bf16[16,16,1664]{2,1,0:T(8,128)(2,1)S(1)} %copy-done, bf16[8,16,1664]{2,1,0:T(8,128)(2,1)S(1)} %collective-permute-done, bf16[8,16,1664]{2,1,0:T(8,128)(2,1)S(1)} %copy-done.1, pred[]{:T(512)S(6)} %lt.3), kind=kLoop, calls=%fused_computation | loop fusion | flops 2981888 | bytes 2555905 | tf_op jit(solution)/shard_map/convert_element_type | solution.py:305
Async XLA Ops:
  43.9 14.4 %collective-permute-start = (bf16[8,16,1664]{2,1,0:T(8,128)(2,1)}, bf16[8,16,1664]{2,1,0:T(8,128)(2,1)S(1)}, u32[]{:S(2)}, u32[]{:S(2)}) collective-permute-start(bf16[8,16,1664]{2,1,0:T(8,128)(2,1)} %get-tuple-element.9), channel_id=1, source_target_pairs={{0,16},{16,0},{1,17},{17,1},{2,18},{18,2},{3,19},{19,3},{4,20},{20... | collective-permute-start | bytes 1277960 | tf_op jit(solution)/shard_map/ppermute | solution.py:299
  45.0 13.2 %copy-start = (bf16[16,16,1664]{2,1,0:T(8,128)(2,1)S(1)}, bf16[16,16,1664]{2,1,0:T(8,128)(2,1)}, u32[]{:S(2)}) copy-start(bf16[16,16,1664]{2,1,0:T(8,128)(2,1)} %get-tuple-element.7) | copy-start | bytes 2555908
  45.0 13.2 %copy-start.1 = (bf16[8,16,1664]{2,1,0:T(8,128)(2,1)S(1)}, bf16[8,16,1664]{2,1,0:T(8,128)(2,1)}, u32[]{:S(2)}) copy-start(bf16[8,16,1664]{2,1,0:T(8,128)(2,1)} %get-tuple-element.8) | copy-start | bytes 1277956
